TPU v7x, 256 devices: a whole 4x4x8 slice. The times are simulated.
256 devices in a mesh: wide: 64 (over x, z, core), narrow: 4 (over y).
Axes of the slice: x: 4, y: 4, z: 8, core: 2. Of those that a mesh axis runs over, the one named last changes fastest.
Arguments:
- queries: bfloat16 [512, 1024], P(('wide', 'narrow')), may hold values from -16 to 16
- archive_keys: bfloat16 [196608, 1024], P(('wide', 'narrow')), may hold values from -6 to 6
- futures: bfloat16 [196608, 1024], P(('wide', 'narrow')), may hold values from -6 to 6
- counts: int32 [256], P(('wide', 'narrow')), may hold values from 256 to 768
- owners: int32 [512], replicated, may hold values from 0 to 511, each once
Outputs:
- forecast: bfloat16 [512, 1024], P(('wide', 'narrow'))
Inputs may be any that keep to these rules, and one draw needn't show every extreme that they name: owners is a permutation of 0 to 511.
All inputs are finite; a program needn't handle non-finite values.
Results may differ from a plain program's by a relative error of at most 0.004.
Values may be sent and summed in bfloat16 or wider, within the bound.
A program may use at most 64 MiB of HBM per device.

v0:
```python
import math

import jax
import jax.numpy as jnp
from jax import lax
from jax.sharding import PartitionSpec as P

score_scale = 3.0


def body(queries, archive_keys, futures, counts, owners):
    shard_rows = archive_keys.shape[0]
    feature_width = archive_keys.shape[1]
    score_factor = score_scale / math.sqrt(feature_width)
    valid_count = counts[0]
    row_index = lax.broadcasted_iota(jnp.int32, (1, shard_rows), 1)
    scores = (
        lax.dot_general(
            lax.all_gather(queries, ("wide", "narrow"), axis=0, tiled=True),
            archive_keys,
            (((1,), (1,)), ((), ())),
            preferred_element_type=jnp.float32,
        )
        * score_factor
    )
    scores = jnp.where(row_index < valid_count, scores, -jnp.inf)
    maxima = lax.pmax(jnp.max(scores, axis=1), ("wide", "narrow"))
    kernel = jnp.where(row_index < valid_count, jnp.exp(scores - maxima[:, None]), 0.0)
    numer = jnp.dot(kernel.astype(jnp.bfloat16), futures, preferred_element_type=jnp.float32)
    denom = jnp.sum(kernel, axis=1)
    numer_mine, denom_mine = (
        lax.psum_scatter(numer[owners], ("wide", "narrow"), scatter_dimension=0, tiled=True),
        lax.psum_scatter(denom[owners], ("wide", "narrow"), scatter_dimension=0, tiled=True),
    )
    analog = numer_mine / denom_mine[:, None]
    norm_factor = lax.rsqrt(jnp.mean(analog * analog, axis=1, keepdims=True) + 1e-06)
    return (analog * norm_factor).astype(jnp.bfloat16)


def solution(mesh):
    placed = (
        P(("wide", "narrow"), None),
        P(("wide", "narrow"), None),
        P(("wide", "narrow"), None),
        P(("wide", "narrow")),
        P(),
    )
    return jax.shard_map(
        body, mesh=mesh, in_specs=placed, out_specs=P(("wide", "narrow"), None), check_vma=False
    )
```

profile of v0, /device:TPU:1, one launch (start us, length us, event | category | flops | bytes accessed | tf_op | source)
XLA Modules:
  0.0 470.7 jit_solution(6443748393197689629)
XLA Ops:
  6.5 0.0 copy-start
  6.5 0.0 all-gather.3.cloned.1.call-start
  6.5 0.7 all-gather.3.cloned.1.call-update
  7.3 0.0 all-reduce.4.cloned.1.call-start
  8.0 0.7 compare_select_fusion
  8.7 108.7 %all-gather.3.cloned.1.call-done = bf16[256,2,1024]{2,1,0:T(2,128)(2,1)} async-done(((bf16[1,2,1024]{2,1,0:T(2,128)(2,1)}), bf16[256,2,1024]{2,1,0:T(2,128)(2,1)}) %all-gather.3.cloned.1.call-update) | async-done | bytes 1048592 | tf_op jit(solution)/shard_map/all_gather | solution.py:19
  117.3 2.3 reshape.34
  119.6 2.8 fusion.8
  122.5 76.8 %pmax.7 = f32[512]{0:T(512)S(1)} all-reduce(f32[512]{0:T(512)S(1)} %get-tuple-element.7), channel_id=1, replica_groups=mesh['wide'=64,'narrow'=4] {'wide','narrow'}, use_global_device_ids=true, to_apply=%region_1.2 | all-reduce | flops 512 | bytes 4096 | tf_op jit(solution)/shard_map/pmax | solution.py:27
  199.2 0.0 copy-done
  199.2 2.4 fusion.2
  201.6 5.3 %gather_fusion = f32[512,1024]{1,0:T(8,128)} fusion(f32[512,1024]{1,0:T(8,128)} %fusion.2, s32[1024]{0:T(1024)S(1)} %pad_clamp_fusion), kind=kCustom, calls=%fused_computation | custom fusion | bytes 4196352 | tf_op jit(solution)/shard_map/gather | solution.py:32
  206.9 0.0 all-reduce.4.cloned.1.call-update
  206.9 0.4 fusion
  207.3 3.5 gather_fusion.1
  210.8 73.1 %all-reduce.1 = f32[512]{0:T(512)S(1)} all-reduce(f32[512]{0:T(512)S(1)} %gather_fusion.1), channel_id=3, replica_groups=mesh['wide'=64,'narrow'=4] {'wide','narrow'}, use_global_device_ids=true, to_apply=%region_4.5.clone | all-reduce | flops 512 | bytes 4096
  284.0 0.1 dynamic-slice.1
  284.0 178.2 %all-reduce.4.cloned.1.call-done = f32[512,1024]{1,0:T(8,128)} async-done(((f32[512,1024]{1,0:T(8,128)}), f32[512,1024]{1,0:T(8,128)}) %all-reduce.4.cloned.1.call-update) | async-done | bytes 2097168
  462.2 0.9 multiply_reduce_fusion
  463.2 0.7 multiply_convert_fusion
  (3 shorter events, 0.0 us)
Async XLA Ops:
  6.5 192.7 %copy-start = (bf16[768,1024]{1,0:T(8,128)(2,1)S(1)}, bf16[768,1024]{1,0:T(8,128)(2,1)}, u32[]{:S(2)}) copy-start(bf16[768,1024]{1,0:T(8,128)(2,1)} %param.7) | copy-start | bytes 4718596
  6.5 110.8 %all-gather.3.cloned.1.call-start = ((), (), s32[]{:S(2)}) async-start(), calls=%async_computation | async-start | bytes 1052672 | tf_op jit(solution)/shard_map/all_gather | solution.py:19
  7.3 455.0 %all-reduce.4.cloned.1.call-start = ((), (), s32[]{:S(2)}) async-start(), calls=%async_computation.1 | async-start | bytes 4194304
Sparse Core Ops, SparseCore 0:
  11.1 106.2 all-gather.2
  207.0 255.1 all-reduce.3
where the time goes:
time: 472 us; the launch traced here: 471 us
  waiting for transfers between devices  288 us (61%)
  blocking collectives  150 us (32%)
  between operations  14.1 us (3%)
  local copies, waits for them, and re-layouts  11.1 us (2%)
  matrix products  5.25 us (1%)
    unnamed x3, waiting for transfers between devices  179 us
    all_gather x1, waiting for transfers between devices, body(): lax.all_gather(queries, ('wide', 'narrow'), axis=0, tiled=True)  109 us
    pmax x1, blocking collectives, body(): maxima = lax.pmax(jnp.max(scores, axis=1), ('wide', 'narrow'))  76.8 us
    unnamed x1, blocking collectives  73.1 us
  transfers between devices with their start and end apart: 2, of which 2 were waited for; matrix products, arithmetic and copies ran while one was open for 1% of the time, Pallas kernels for 0%

commit v1 on v0

v1 whole, which is shorter than its diff:
```python
import jax
import jax.numpy as jnp
from jax import lax
from jax.experimental import pallas as pl
from jax.experimental.pallas import tpu as pltpu
from jax.sharding import PartitionSpec as P

MESH = pl.DeviceIdType.MESH

NX, NY, NZ = 4, 4, 8
PLANE = NX * NY
ROWS = 2 * NZ
MINE = PLANE * ROWS
WIDTH = 1024
HALF = 512
STATS = 128
ARCHIVE = 768
TILE = 256

score_scale = 3.0
exponent_factor = score_scale / 32.0 * 1.4426950408889634


def natural_row(core, position):
    x, y = position // 64, (position // 16) % 4
    z, row = (position // 2) % 8, position % 2
    return x * 128 + z * 16 + core * 8 + y * 2 + row


def kernel(
    queries,
    keys_hbm,
    futures_hbm,
    counts,
    owners,
    out,
    zgather,
    gather32,
    gathered,
    keys,
    futures,
    limits,
    onehot,
    scores,
    weights,
    part_send,
    part_recv,
    zpart_send,
    zpart_recv,
    local_sem,
    archive_send,
    archive_recv,
    zg_send,
    zg_recv,
    pg_send,
    pg_recv,
    fw_send,
    fw_recv,
    ps_send,
    ps_recv,
    zs_send,
    zs_recv,
):
    wide, y = lax.axis_index("wide"), lax.axis_index("narrow")
    x, z, core = wide // 16, (wide // 2) % 8, wide % 2
    plane = x * NY + y

    def device(x, y, z, core):
        return {"wide": (x * NZ + z) * 2 + core, "narrow": y}

    def z_peer(step):
        other = (z + step) % NZ
        return other, device(x, y, other, core)

    def plane_peer(step):
        other_x, other_y = (x + step // NY) % NX, (y + step % NY) % NY
        return other_x * NY + other_y, device(other_x, other_y, z, core)

    twin = device(x, y, z, 1 - core)

    def remote(src, dst, send, recv, target):
        return pltpu.make_async_remote_copy(
            src_ref=src, dst_ref=dst, send_sem=send, recv_sem=recv, device_id=target, device_id_type=MESH
        )

    own_keys = pltpu.make_async_copy(keys_hbm, keys.at[0], local_sem.at[0])
    own_futures = pltpu.make_async_copy(futures_hbm, futures.at[0], local_sem.at[1])
    own_keys.start()
    own_futures.start()

    barrier = pltpu.get_barrier_semaphore()

    def greet_z(step, carry):
        pl.semaphore_signal(barrier, inc=1, device_id=z_peer(step)[1], device_id_type=MESH)
        return carry

    def greet_plane(step, carry):
        pl.semaphore_signal(barrier, inc=1, device_id=plane_peer(step)[1], device_id_type=MESH)
        return carry

    lax.fori_loop(1, NZ, greet_z, 0)
    lax.fori_loop(1, PLANE, greet_plane, 0)
    pl.semaphore_signal(barrier, inc=1, device_id=twin, device_id_type=MESH)
    zgather[z] = queries[...].astype(jnp.float32)
    limits[0] = jnp.full((8, 128), counts[0], jnp.int32).astype(jnp.float32)
    pl.semaphore_wait(barrier, NZ - 1 + PLANE - 1 + 1)

    def zg_copy(step):
        other, target = z_peer(step)
        return remote(zgather.at[z], zgather.at[z], zg_send.at[step], zg_recv.at[z], target)

    def zg_start(step, carry):
        zg_copy(step).start()
        return carry

    lax.fori_loop(1, NZ, zg_start, 0)

    to_twin = (
        remote(limits.at[0], limits.at[1], archive_send.at[2], archive_recv.at[2], twin),
        remote(keys_hbm, keys.at[1], archive_send.at[0], archive_recv.at[0], twin),
        remote(futures_hbm, futures.at[1], archive_send.at[1], archive_recv.at[1], twin),
    )
    for copy in to_twin:
        copy.start()

    position = lax.broadcasted_iota(jnp.int32, (1, 2 * MINE), 1)
    held = natural_row(position // MINE, position % MINE)
    lane = lax.broadcasted_iota(jnp.int32, (64, 128), 1)
    wanted = natural_row(core, lax.broadcasted_iota(jnp.int32, (64, 128), 0))
    for block in range(NX):
        picked = jnp.where(lane == wanted, owners[block : block + 1, :].astype(jnp.float32), 0.0)
        owner = jnp.sum(picked, axis=1, keepdims=True)
        onehot[block * 64 : block * 64 + 64, :] = jnp.where(
            owner == held.astype(jnp.float32), 1.0, 0.0
        ).astype(jnp.bfloat16)

    def zg_wait(step, carry):
        other, target = z_peer(step)
        remote(zgather.at[other], zgather.at[other], zg_send.at[step], zg_recv.at[other], target).wait_recv()
        return carry

    lax.fori_loop(1, NZ, zg_wait, 0)
    for k in range(NZ):
        gather32[2 * k : 2 * k + 2, :] = zgather[k]
    gathered[core, plane] = gather32[...].astype(jnp.bfloat16)

    def pg_start(step, carry):
        other, target = plane_peer(step)
        block = gathered.at[core, plane]
        remote(block, block, pg_send.at[step], pg_recv.at[plane], target).start()
        return carry

    lax.fori_loop(1, PLANE, pg_start, 0)

    def fw_copy(other):
        block = gathered.at[core, other]
        return remote(block, block, fw_send.at[other], fw_recv.at[other], twin)

    fw_copy(plane).start()

    def pg_wait(step, carry):
        other, target = plane_peer(step)
        block = gathered.at[core, other]
        remote(block, block, pg_send.at[step], pg_recv.at[other], target).wait_recv()
        fw_copy(other).start()
        return carry

    lax.fori_loop(1, PLANE, pg_wait, 0)

    own_keys.wait()
    own_futures.wait()
    for copy in to_twin:
        copy.wait()

    def fw_wait(other, carry):
        block = gathered.at[1 - core, other]
        remote(block, block, fw_send.at[other], fw_recv.at[other], twin).wait_recv()
        return carry

    lax.fori_loop(0, PLANE, fw_wait, 0)

    every = gathered[...].reshape(2 * MINE, WIDTH)
    mine = jnp.dot(onehot[...], every, preferred_element_type=jnp.float32).astype(jnp.bfloat16)

    column = lax.broadcasted_iota(jnp.int32, (1, TILE), 1).astype(jnp.float32)
    best = None
    for half in range(2):
        limit = limits[half, 0:1, 0:1]
        for tile in range(ARCHIVE // TILE):
            part = lax.dot_general(
                mine,
                keys[half, tile * TILE : (tile + 1) * TILE, :],
                (((1,), (1,)), ((), ())),
                preferred_element_type=jnp.float32,
            )
            part = jnp.where(column + float(tile * TILE) < limit, part, -1e30)
            at = half * ARCHIVE + tile * TILE
            scores[:, at : at + TILE] = part
            top = jnp.max(part, axis=1, keepdims=True)
            best = top if best is None else jnp.maximum(best, top)
    best = best.astype(jnp.bfloat16).astype(jnp.float32)
    total = jnp.zeros((MINE, 1), jnp.float32)
    for tile in range(2 * ARCHIVE // TILE):
        span = slice(tile * TILE, (tile + 1) * TILE)
        weight = jnp.exp2((scores[:, span] - best) * exponent_factor)
        weights[:, span] = weight.astype(jnp.bfloat16)
        total = total + jnp.sum(weight, axis=1, keepdims=True)

    stat_lane = lax.broadcasted_iota(jnp.int32, (1, STATS), 1)
    high = total.astype(jnp.bfloat16).astype(jnp.float32)
    stats = jnp.where(stat_lane < 32, best, jnp.where(stat_lane < 64, high, total - high))
    part_send[:, :, WIDTH:] = stats.astype(jnp.bfloat16).reshape(PLANE, ROWS, STATS)
    for half in range(2):
        span = slice(half * HALF, (half + 1) * HALF)
        sums = None
        for side in range(2):
            term = jnp.dot(
                weights[:, side * ARCHIVE : (side + 1) * ARCHIVE],
                futures[side, :, span],
                preferred_element_type=jnp.float32,
            )
            sums = term if sums is None else sums + term
        part_send[:, :, span] = sums.astype(jnp.bfloat16).reshape(PLANE, ROWS, HALF)

    def ps_start(step, carry):
        other, target = plane_peer(step)
        remote(part_send.at[other], part_recv.at[plane], ps_send.at[step], ps_recv.at[plane], target).start()
        return carry

    lax.fori_loop(1, PLANE, ps_start, 0)
    part_recv[plane] = part_send[plane]

    def ps_wait(step, carry):
        other, target = plane_peer(step)
        remote(part_send.at[other], part_recv.at[other], ps_send.at[step], ps_recv.at[other], target).wait_recv()
        return carry

    lax.fori_loop(1, PLANE, ps_wait, 0)

    best = part_recv[0, :, WIDTH : WIDTH + 1].astype(jnp.float32)
    for k in range(1, PLANE):
        best = jnp.maximum(best, part_recv[k, :, WIDTH : WIDTH + 1].astype(jnp.float32))
    sums = jnp.zeros((ROWS, WIDTH), jnp.float32)
    total = jnp.zeros((ROWS, 1), jnp.float32)
    for k in range(PLANE):
        stats = part_recv[k, :, WIDTH:].astype(jnp.float32)
        scale = jnp.exp2((stats[:, 0:1] - best) * exponent_factor)
        sums = sums + part_recv[k, :, :WIDTH].astype(jnp.float32) * scale
        total = total + (stats[:, 32:33] + stats[:, 64:65]) * scale
    stats = jnp.where(stat_lane < 64, best, total)
    for k in range(NZ):
        zpart_send[k, :, :WIDTH] = sums[2 * k : 2 * k + 2, :]
        zpart_send[k, :, WIDTH:] = stats[2 * k : 2 * k + 2, :]

    def zs_start(step, carry):
        other, target = z_peer(step)
        remote(zpart_send.at[other], zpart_recv.at[z], zs_send.at[step], zs_recv.at[z], target).start()
        return carry

    lax.fori_loop(1, NZ, zs_start, 0)
    zpart_recv[z] = zpart_send[z]

    def zs_wait(step, carry):
        other, target = z_peer(step)
        remote(zpart_send.at[other], zpart_recv.at[other], zs_send.at[step], zs_recv.at[other], target).wait_recv()
        return carry

    lax.fori_loop(1, NZ, zs_wait, 0)

    best = zpart_recv[0, :, WIDTH : WIDTH + 1]
    for k in range(1, NZ):
        best = jnp.maximum(best, zpart_recv[k, :, WIDTH : WIDTH + 1])
    sums = jnp.zeros((2, WIDTH), jnp.float32)
    total = jnp.zeros((2, 1), jnp.float32)
    for k in range(NZ):
        stats = zpart_recv[k, :, WIDTH:]
        scale = jnp.exp2((stats[:, 0:1] - best) * exponent_factor)
        sums = sums + zpart_recv[k, :, :WIDTH] * scale
        total = total + stats[:, 64:65] * scale
    analog = sums / total
    norm_factor = lax.rsqrt(jnp.mean(analog * analog, axis=1, keepdims=True) + 1e-06)
    out[...] = (analog * norm_factor).astype(jnp.bfloat16)

    def z_sent(step, carry):
        other, target = z_peer(step)
        zg_copy(step).wait_send()
        remote(zpart_send.at[other], zpart_recv.at[z], zs_send.at[step], zs_recv.at[z], target).wait_send()
        return carry

    def plane_sent(step, carry):
        other, target = plane_peer(step)
        block = gathered.at[core, plane]
        remote(block, block, pg_send.at[step], pg_recv.at[plane], target).wait_send()
        remote(part_send.at[other], part_recv.at[plane], ps_send.at[step], ps_recv.at[plane], target).wait_send()
        return carry

    def fw_sent(other, carry):
        fw_copy(other).wait_send()
        return carry

    lax.fori_loop(1, NZ, z_sent, 0)
    lax.fori_loop(1, PLANE, plane_sent, 0)
    lax.fori_loop(0, PLANE, fw_sent, 0)


def body(queries, archive_keys, futures, counts, owners):
    vmem = pl.BlockSpec(memory_space=pltpu.VMEM)
    smem = pl.BlockSpec(memory_space=pltpu.SMEM)
    anywhere = pl.BlockSpec(memory_space=pl.ANY)
    dma = pltpu.SemaphoreType.DMA
    return pl.pallas_call(
        kernel,
        out_shape=jax.ShapeDtypeStruct((2, WIDTH), jnp.bfloat16),
        in_specs=[vmem, anywhere, anywhere, smem, vmem],
        out_specs=vmem,
        scratch_shapes=[
            pltpu.VMEM((NZ, 2, WIDTH), jnp.float32),
            pltpu.VMEM((ROWS, WIDTH), jnp.float32),
            pltpu.VMEM((2, PLANE, ROWS, WIDTH), jnp.bfloat16),
            pltpu.VMEM((2, ARCHIVE, WIDTH), jnp.bfloat16),
            pltpu.VMEM((2, ARCHIVE, WIDTH), jnp.bfloat16),
            pltpu.VMEM((2, 8, 128), jnp.float32),
            pltpu.VMEM((MINE, 2 * MINE), jnp.bfloat16),
            pltpu.VMEM((MINE, 2 * ARCHIVE), jnp.float32),
            pltpu.VMEM((MINE, 2 * ARCHIVE), jnp.bfloat16),
            pltpu.VMEM((PLANE, ROWS, WIDTH + STATS), jnp.bfloat16),
            pltpu.VMEM((PLANE, ROWS, WIDTH + STATS), jnp.bfloat16),
            pltpu.VMEM((NZ, 2, WIDTH + STATS), jnp.float32),
            pltpu.VMEM((NZ, 2, WIDTH + STATS), jnp.float32),
            dma((2,)),
            dma((3,)),
            dma((3,)),
            dma((NZ,)),
            dma((NZ,)),
            dma((PLANE,)),
            dma((PLANE,)),
            dma((PLANE,)),
            dma((PLANE,)),
            dma((PLANE,)),
            dma((PLANE,)),
            dma((NZ,)),
            dma((NZ,)),
        ],
        compiler_params=pltpu.CompilerParams(
            collective_id=0, has_side_effects=True, vmem_limit_bytes=40 * 2**20
        ),
        name="analog_forecast",
    )(queries, archive_keys, futures, counts, owners.reshape(4, 128))


def solution(mesh):
    rows = P(("wide", "narrow"), None)
    return jax.shard_map(
        body,
        mesh=mesh,
        in_specs=(rows, rows, rows, P(("wide", "narrow")), P()),
        out_specs=rows,
        check_vma=False,
    )
```

time: 472 us -> 48.4 us (0.10)
  waiting for transfers between devices: 288 us -> 0 us
  blocking collectives: 150 us -> 0 us
  Pallas kernels: 0 us -> 42.7 us
  between operations: 14.1 us -> 0.67 us
  local copies, waits for them, and re-layouts: 11.1 us -> 4.77 us
  matrix products: 5.25 us -> 0 us
    unnamed x3 -> x0, waiting for transfers between devices: 179 us -> none
    all_gather x1 -> x0, waiting for transfers between devices: 109 us -> none  [body(): lax.all_gather(queries, ('wide', 'narrow'), axis=0, tiled=True)]
    pmax x1 -> x0, blocking collectives: 76.8 us -> none  [body(): maxima = lax.pmax(jnp.max(scores, axis=1), ('wide', 'narrow'))]
    unnamed x1 -> x0, blocking collectives: 73.1 us -> none
    pallas_call x0 -> x1, Pallas kernels: none -> 42.7 us  [body(): pl.pallas_call(kernel, out_shape=jax.ShapeDtypeStruct((2, WIDTH), jnp.bfl...]
    gather x2 -> x0, local copies, waits for them, and re-layouts: 8.74 us -> none  [the longest x1 5.25 us: body(): numer[owners]]
    dot_general x2 -> x0, matrix products: 5.25 us -> none  [the longest x1 2.84 us: body(): lax.dot_general(lax.all_gather(queries, ('wide', 'narrow'), axis=0, tiled...]
  transfers between devices with their start and end apart: 2 -> 0, of which waited for: 2 -> 0; matrix products, arithmetic and copies ran while one was open for 1% -> 0% of each run, Pallas kernels for 0% -> 0%
where the time goes in v1:
time: 48.4 us; the launch traced here: 48.2 us
  Pallas kernels  42.7 us (88%)
  local copies, waits for them, and re-layouts  4.77 us (10%)
  between operations  0.67 us (1%)
    pallas_call x1, Pallas kernels, body(): pl.pallas_call(kernel, out_shape=jax.ShapeDtypeStruct((2, WIDTH), jnp.bfl...  42.7 us
    unnamed x9, local copies, waits for them, and re-layouts  4.77 us

profile of v1, /device:TPU:1, one launch (start us, length us, event | category | flops | bytes accessed | tf_op | source)
XLA Modules:
  0.0 48.2 jit_solution(17202055981796491888)
XLA Ops:
  0.7 0.0 copy-start
  0.7 1.4 %copy-done = bf16[768,1024]{1,0:T(8,128)(2,1)S(1)} copy-done((bf16[768,1024]{1,0:T(8,128)(2,1)S(1)}, bf16[768,1024]{1,0:T(8,128)(2,1)}, u32[]{:S(2)}) %copy-start) | copy-done | bytes 1572888
  2.1 0.0 copy-start.1
  2.1 1.4 %copy-done.1 = bf16[768,1024]{1,0:T(8,128)(2,1)S(1)} copy-done((bf16[768,1024]{1,0:T(8,128)(2,1)S(1)}, bf16[768,1024]{1,0:T(8,128)(2,1)}, u32[]{:S(2)}) %copy-start.1) | copy-done | bytes 1572888
  3.5 0.0 copy-start.2
  3.5 0.7 %copy-done.2 = bf16[2,1024]{1,0:T(2,128)(2,1)S(1)} copy-done((bf16[2,1024]{1,0:T(2,128)(2,1)S(1)}, bf16[2,1024]{1,0:T(2,128)(2,1)}, u32[]{:S(2)}) %copy-start.2) | copy-done | bytes 4120
  4.2 0.0 copy-start.3
  4.2 0.7 %copy-done.3 = s32[512]{0:T(512)S(1)} copy-done((s32[512]{0:T(512)S(1)}, s32[512]{0:T(512)}, u32[]{:S(2)}) %copy-start.3) | copy-done | bytes 2072
  4.8 42.7 %analog_forecast.1 = bf16[2,1024]{1,0:T(2,128)(2,1)S(1)} custom-call(bf16[2,1024]{1,0:T(2,128)(2,1)S(1)} %copy-done.2, bf16[768,1024]{1,0:T(8,128)(2,1)S(1)} %copy-done, bf16[768,1024]{1,0:T(8,128)(2,1)S(1)} %copy-done.1, s32[1]{0:T(128)S(6)} %copy.7.counts, s32[4,128]{1,0:T(4,128)S(1)} %bitcast.1), custom_call_target="tpu_custom_call" | custom-call | tf_op jit(solution)/shard_map/analog_forecast/pallas_call | solution.py:311
  47.6 0.6 %copy.8 = bf16[2,1024]{1,0:T(2,128)(2,1)} copy(bf16[2,1024]{1,0:T(2,128)(2,1)S(1)} %analog_forecast.1) | data formatting | bytes 8192
Async XLA Ops:
  0.7 1.4 %copy-start = (bf16[768,1024]{1,0:T(8,128)(2,1)S(1)}, bf16[768,1024]{1,0:T(8,128)(2,1)}, u32[]{:S(2)}) copy-start(bf16[768,1024]{1,0:T(8,128)(2,1)} %keys_hbm.1) | copy-start | bytes 4718596
  2.1 1.4 %copy-start.1 = (bf16[768,1024]{1,0:T(8,128)(2,1)S(1)}, bf16[768,1024]{1,0:T(8,128)(2,1)}, u32[]{:S(2)}) copy-start(bf16[768,1024]{1,0:T(8,128)(2,1)} %futures_hbm.1) | copy-start | bytes 4718596
  3.5 0.7 %copy-start.2 = (bf16[2,1024]{1,0:T(2,128)(2,1)S(1)}, bf16[2,1024]{1,0:T(2,128)(2,1)}, u32[]{:S(2)}) copy-start(bf16[2,1024]{1,0:T(2,128)(2,1)} %queries.1) | copy-start | bytes 12292
  4.2 0.7 %copy-start.3 = (s32[512]{0:T(512)S(1)}, s32[512]{0:T(512)}, u32[]{:S(2)}) copy-start(s32[512]{0:T(512)} %param.9) | copy-start | bytes 6148

commit v2 on v1

v2 whole, which is shorter than its diff:
```python
import jax
import jax.numpy as jnp
from jax import lax
from jax.experimental import pallas as pl
from jax.experimental.pallas import tpu as pltpu
from jax.sharding import PartitionSpec as P

MESH = pl.DeviceIdType.MESH

NX, NY, NZ = 4, 4, 8
PLANE = NX * NY
ROWS = 16
MINE = PLANE * ROWS
GROUP = MINE // 2
WIDTH = 1024
HALF = 512
STATS = 128
ARCHIVE = 768
TILE = 256

NEAR, FAR = (0, 1, 7, 6), (4, 3, 5, 2)
OFFSETS = NEAR, FAR

STEPS = sorted(
    [(a, b) for a in range(NX) for b in range(NY) if a or b],
    key=lambda s: -(min(s[0], NX - s[0]) + min(s[1], NY - s[1])),
)

score_scale = 3.0
exponent_factor = score_scale / 32.0 * 1.4426950408889634


def pick(index, values):
    result = jnp.full_like(index, values[0])
    for k in range(1, len(values)):
        result = jnp.where(index == k, values[k], result)
    return result


def natural_row(x, y, z, core, row):
    return x * 128 + z * 16 + core * 8 + y * 2 + row


def kernel(
    queries_hbm,
    keys_hbm,
    futures_hbm,
    counts_hbm,
    owners_hbm,
    out,
    queries,
    counts,
    owners,
    own32,
    zgather,
    gather32,
    gathered,
    keys,
    futures,
    limits,
    onehot,
    scores,
    weights,
    far_send,
    far_recv,
    near_send,
    near_recv,
    zpart_send,
    zpart_recv,
    local_sem,
    archive_send,
    archive_recv,
    zg_send,
    zg_recv,
    pg_send,
    pg_recv,
    fw_send,
    fw_recv,
    ps_send,
    ps_recv,
    zs_send,
    zs_recv,
):
    wide, y = lax.axis_index("wide"), lax.axis_index("narrow")
    x, z, core = wide // 16, (wide // 2) % 8, wide % 2
    plane = x * NY + y

    def device(x, y, z, core):
        return {"wide": (x * NZ + z) * 2 + core, "narrow": y}

    def plane_peer(step):
        other_x, other_y = (x + step[0]) % NX, (y + step[1]) % NY
        return other_x * NY + other_y, device(other_x, other_y, z, core)

    twin = device(x, y, z, 1 - core)

    def remote(src, dst, send, recv, target):
        return pltpu.make_async_remote_copy(
            src_ref=src, dst_ref=dst, send_sem=send, recv_sem=recv, device_id=target, device_id_type=MESH
        )

    loads = [
        pltpu.make_async_copy(src, dst, local_sem.at[k])
        for k, (src, dst) in enumerate(
            [
                (queries_hbm, queries),
                (counts_hbm, counts),
                (owners_hbm, owners),
                (keys_hbm, keys.at[0]),
                (futures_hbm, futures.at[0]),
            ]
        )
    ]
    for load in loads:
        load.start()

    barrier = pltpu.get_barrier_semaphore()
    for step in (4, 3, 5, 2, 6, 1, 7):
        for side in range(2):
            pl.semaphore_signal(
                barrier, inc=1, device_id=device(x, y, (z + step) % NZ, side), device_id_type=MESH
            )
    for step in STEPS:
        pl.semaphore_signal(barrier, inc=1, device_id=plane_peer(step)[1], device_id_type=MESH)
    pl.semaphore_signal(barrier, inc=1, device_id=twin, device_id_type=MESH)
    loads[0].wait()
    own32[...] = queries[...].astype(jnp.float32)
    loads[1].wait()
    limits[0] = jnp.full((8, 128), counts[0], jnp.int32).astype(jnp.float32)
    pl.semaphore_wait(barrier, 2 * (NZ - 1) + PLANE - 1 + 1)

    zg_sends = []
    for step in (4, 3, 5, 2, 6, 1, 7):
        offset = (NZ - step) % NZ
        side = 0 if offset in NEAR else 1
        slot = OFFSETS[side].index(offset) * 2 + core
        copy = remote(
            own32, zgather.at[slot], zg_send.at[step], zg_recv.at[slot], device(x, y, (z + step) % NZ, side)
        )
        copy.start()
        zg_sends.append(copy)
    to_core0 = remote(own32, zgather.at[1], zg_send.at[0], zg_recv.at[1], device(x, y, z, 0))

    @pl.when(core == 1)
    def _():
        to_core0.start()

    @pl.when(core == 0)
    def _():
        zgather[0] = own32[...]

    to_twin = (
        remote(limits.at[0], limits.at[1], archive_send.at[2], archive_recv.at[2], twin),
        remote(keys_hbm, keys.at[1], archive_send.at[0], archive_recv.at[0], twin),
        remote(futures_hbm, futures.at[1], archive_send.at[1], archive_recv.at[1], twin),
    )
    for copy in to_twin:
        copy.start()

    loads[2].wait()
    position = lax.broadcasted_iota(jnp.int32, (1, MINE), 1)
    lane = lax.broadcasted_iota(jnp.int32, (32, 128), 1)
    row = lax.broadcasted_iota(jnp.int32, (32, 128), 0)
    for group in range(2):
        wanted = natural_row(0, row // 8, (z + pick((row // 2) % 4, OFFSETS[1 - group])) % NZ, core, row % 2)
        for block in range(NX):
            picked = jnp.where(lane == wanted, owners[block : block + 1, :].astype(jnp.float32), 0.0)
            owner = jnp.sum(picked, axis=1, keepdims=True)
            at = group * GROUP + block * 32
            for side in range(2):
                held = natural_row(
                    position // 64,
                    (position // 16) % 4,
                    (z + pick((position // 4) % 4, OFFSETS[side])) % NZ,
                    (position // 2) % 2,
                    position % 2,
                )
                onehot[side, at : at + 32, :] = jnp.where(
                    owner == held.astype(jnp.float32), 1.0, 0.0
                ).astype(jnp.bfloat16)

    def zg_wait(slot):
        remote(own32, zgather.at[slot], zg_send.at[0], zg_recv.at[slot], twin).wait_recv()

    for slot in range(1, 8):
        zg_wait(slot)

    @pl.when(core == 1)
    def _():
        zg_wait(0)

    for slot in range(8):
        gather32[2 * slot : 2 * slot + 2, :] = zgather[slot]
    gathered[core, plane] = gather32[...].astype(jnp.bfloat16)

    pg_sends = []
    for k, step in enumerate(STEPS):
        other, target = plane_peer(step)
        block = gathered.at[core, plane]
        copy = remote(block, block, pg_send.at[k], pg_recv.at[plane], target)
        copy.start()
        pg_sends.append(copy)

    def fw_copy(other):
        block = gathered.at[core, other]
        return remote(block, block, fw_send.at[other], fw_recv.at[other], twin)

    fw_copy(plane).start()
    for step in reversed(STEPS):
        other, target = plane_peer(step)
        block = gathered.at[core, other]
        remote(block, block, pg_send.at[0], pg_recv.at[other], target).wait_recv()
        fw_copy(other).start()

    every = gathered[core].reshape(MINE, WIDTH)
    mine = jnp.dot(onehot[core], every, preferred_element_type=jnp.float32)

    for load in loads[3:]:
        load.wait()
    for copy in to_twin:
        copy.wait()

    def fw_wait(other, carry):
        block = gathered.at[1 - core, other]
        remote(block, block, fw_send.at[other], fw_recv.at[other], twin).wait_recv()
        return carry

    lax.fori_loop(0, PLANE, fw_wait, 0)

    every = gathered[1 - core].reshape(MINE, WIDTH)
    mine = (mine + jnp.dot(onehot[1 - core], every, preferred_element_type=jnp.float32)).astype(jnp.bfloat16)

    column = lax.broadcasted_iota(jnp.int32, (1, TILE), 1).astype(jnp.float32)
    best = None
    for half in range(2):
        limit = limits[half, 0:1, 0:1]
        for tile in range(ARCHIVE // TILE):
            part = lax.dot_general(
                mine,
                keys[half, tile * TILE : (tile + 1) * TILE, :],
                (((1,), (1,)), ((), ())),
                preferred_element_type=jnp.float32,
            )
            part = jnp.where(column + float(tile * TILE) < limit, part, -1e30)
            at = half * ARCHIVE + tile * TILE
            scores[:, at : at + TILE] = part
            top = jnp.max(part, axis=1, keepdims=True)
            best = top if best is None else jnp.maximum(best, top)
    best = best.astype(jnp.bfloat16).astype(jnp.float32)
    total = jnp.zeros((MINE, 1), jnp.float32)
    for tile in range(2 * ARCHIVE // TILE):
        span = slice(tile * TILE, (tile + 1) * TILE)
        weight = jnp.exp2((scores[:, span] - best) * exponent_factor)
        weights[:, span] = weight.astype(jnp.bfloat16)
        total = total + jnp.sum(weight, axis=1, keepdims=True)

    stat_lane = lax.broadcasted_iota(jnp.int32, (1, STATS), 1)
    high = total.astype(jnp.bfloat16).astype(jnp.float32)
    stats = jnp.where(stat_lane < 32, best, jnp.where(stat_lane < 64, high, total - high))
    stats = stats.reshape(2, PLANE, 8, STATS)
    stats = jnp.stack([stats[0], stats[1]], axis=1).reshape(MINE, STATS)
    far_send[:, :, HALF:] = stats.astype(jnp.bfloat16).reshape(PLANE, ROWS, STATS)

    ps_sends = []
    for group, (send, recv) in enumerate(((far_send, far_recv), (near_send, near_recv))):
        halves = []
        for half in range(2):
            span = slice(half * HALF, (half + 1) * HALF)
            sums = None
            for side in range(2):
                term = jnp.dot(
                    weights[group * GROUP : (group + 1) * GROUP, side * ARCHIVE : (side + 1) * ARCHIVE],
                    futures[side, :, span],
                    preferred_element_type=jnp.float32,
                )
                sums = term if sums is None else sums + term
            halves.append(sums.reshape(PLANE, 8, HALF))
        sums = jnp.stack(halves, axis=1).reshape(MINE, HALF)
        send[:, :, :HALF] = sums.astype(jnp.bfloat16).reshape(PLANE, ROWS, HALF)
        for k, step in enumerate(STEPS):
            other, target = plane_peer(step)
            copy = remote(send.at[other], recv.at[plane], ps_send.at[group, k], ps_recv.at[group, plane], target)
            copy.start()
            ps_sends.append(copy)
        recv[plane] = send[plane]

    zs_sends = []
    for group, (send, recv) in enumerate(((far_send, far_recv), (near_send, near_recv))):
        for step in STEPS:
            other, target = plane_peer(step)
            remote(send.at[other], recv.at[other], ps_send.at[group, 0], ps_recv.at[group, other], target).wait_recv()
        if group == 0:
            stats = [recv[k, :, HALF:].astype(jnp.float32) for k in range(PLANE)]
            best = stats[0][:, 0:1]
            for k in range(1, PLANE):
                best = jnp.maximum(best, stats[k][:, 0:1])
            scales = [jnp.exp2((s[:, 0:1] - best) * exponent_factor) for s in stats]
            total = jnp.zeros((ROWS, 1), jnp.float32)
            for k in range(PLANE):
                total = total + (stats[k][:, 32:33] + stats[k][:, 64:65]) * scales[k]
            passed = jnp.where(stat_lane < 64, best, total)
        sums = jnp.zeros((ROWS, HALF), jnp.float32)
        for k in range(PLANE):
            scale = scales[k][group * 8 : group * 8 + 8]
            scale = jnp.concatenate([scale, scale], axis=0)
            sums = sums + recv[k, :, :HALF].astype(jnp.float32) * scale
        for index, offset in enumerate(OFFSETS[1 - group]):
            slot = group * 4 + index
            zpart_send[slot, :, :HALF] = sums[2 * index : 2 * index + 2, :]
            zpart_send[slot, :, HALF:WIDTH] = sums[8 + 2 * index : 8 + 2 * index + 2, :]
            zpart_send[slot, :, WIDTH:] = passed[group * 8 + 2 * index : group * 8 + 2 * index + 2, :]
        for index, offset in enumerate(OFFSETS[1 - group]):
            slot = group * 4 + index
            if offset == 0:
                zpart_recv[z] = zpart_send[slot]
            else:
                copy = remote(
                    zpart_send.at[slot],
                    zpart_recv.at[z],
                    zs_send.at[offset],
                    zs_recv.at[z],
                    device(x, y, (z + offset) % NZ, core),
                )
                copy.start()
                zs_sends.append(copy)

    for step in range(1, NZ):
        other = (z + step) % NZ
        remote(zpart_send.at[0], zpart_recv.at[other], zs_send.at[0], zs_recv.at[other], twin).wait_recv()

    best = zpart_recv[0, :, WIDTH : WIDTH + 1]
    for k in range(1, NZ):
        best = jnp.maximum(best, zpart_recv[k, :, WIDTH : WIDTH + 1])
    sums = jnp.zeros((2, WIDTH), jnp.float32)
    total = jnp.zeros((2, 1), jnp.float32)
    for k in range(NZ):
        stats = zpart_recv[k, :, WIDTH:]
        scale = jnp.exp2((stats[:, 0:1] - best) * exponent_factor)
        sums = sums + zpart_recv[k, :, :WIDTH] * scale
        total = total + stats[:, 64:65] * scale
    analog = sums / total
    norm_factor = lax.rsqrt(jnp.mean(analog * analog, axis=1, keepdims=True) + 1e-06)
    out[...] = (analog * norm_factor).astype(jnp.bfloat16)

    for copy in zg_sends + pg_sends + ps_sends + zs_sends:
        copy.wait_send()

    @pl.when(core == 1)
    def _():
        to_core0.wait_send()

    def fw_sent(other, carry):
        fw_copy(other).wait_send()
        return carry

    lax.fori_loop(0, PLANE, fw_sent, 0)


def body(queries, archive_keys, futures, counts, owners):
    hbm = pl.BlockSpec(memory_space=pltpu.HBM)
    dma = pltpu.SemaphoreType.DMA
    bf16, f32 = jnp.bfloat16, jnp.float32
    return pl.pallas_call(
        kernel,
        out_shape=jax.ShapeDtypeStruct((2, WIDTH), bf16),
        in_specs=[hbm] * 5,
        out_specs=pl.BlockSpec(memory_space=pltpu.VMEM),
        scratch_shapes=[
            pltpu.VMEM((2, WIDTH), bf16),
            pltpu.SMEM((1,), jnp.int32),
            pltpu.VMEM((4, 128), jnp.int32),
            pltpu.VMEM((2, WIDTH), f32),
            pltpu.VMEM((8, 2, WIDTH), f32),
            pltpu.VMEM((ROWS, WIDTH), f32),
            pltpu.VMEM((2, PLANE, ROWS, WIDTH), bf16),
            pltpu.VMEM((2, ARCHIVE, WIDTH), bf16),
            pltpu.VMEM((2, ARCHIVE, WIDTH), bf16),
            pltpu.VMEM((2, 8, 128), f32),
            pltpu.VMEM((2, MINE, MINE), bf16),
            pltpu.VMEM((MINE, 2 * ARCHIVE), f32),
            pltpu.VMEM((MINE, 2 * ARCHIVE), bf16),
            pltpu.VMEM((PLANE, ROWS, HALF + STATS), bf16),
            pltpu.VMEM((PLANE, ROWS, HALF + STATS), bf16),
            pltpu.VMEM((PLANE, ROWS, HALF), bf16),
            pltpu.VMEM((PLANE, ROWS, HALF), bf16),
            pltpu.VMEM((NZ, 2, WIDTH + STATS), f32),
            pltpu.VMEM((NZ, 2, WIDTH + STATS), f32),
            dma((5,)),
            dma((3,)),
            dma((3,)),
            dma((NZ,)),
            dma((NZ,)),
            dma((PLANE,)),
            dma((PLANE,)),
            dma((PLANE,)),
            dma((PLANE,)),
            dma((2, PLANE)),
            dma((2, PLANE)),
            dma((NZ,)),
            dma((NZ,)),
        ],
        compiler_params=pltpu.CompilerParams(
            collective_id=0, has_side_effects=True, vmem_limit_bytes=60 * 2**20
        ),
        name="analog_forecast",
    )(queries, archive_keys, futures, counts, owners.reshape(4, 128))


def solution(mesh):
    rows = P(("wide", "narrow"), None)
    return jax.shard_map(
        body,
        mesh=mesh,
        in_specs=(rows, rows, rows, P(("wide", "narrow")), P()),
        out_specs=rows,
        check_vma=False,
    )
```

time: 48.4 us -> 43.1 us (0.89)
  local copies, waits for them, and re-layouts: 4.77 us -> 1.28 us
  Pallas kernels: 42.7 us -> 41 us
    unnamed x9 -> x1, local copies, waits for them, and re-layouts: 4.77 us -> 1.28 us
    pallas_call x1, Pallas kernels: 42.7 us -> 41 us  [body(): pl.pallas_call(kernel, out_shape=jax.ShapeDtypeStruct((2, WIDTH), bf16),...]
where the time goes in v2:
time: 43.1 us; the launch traced here: 43 us
  Pallas kernels  41 us (95%)
  local copies, waits for them, and re-layouts  1.28 us (3%)
  between operations  0.66 us (2%)
    pallas_call x1, Pallas kernels, body(): pl.pallas_call(kernel, out_shape=jax.ShapeDtypeStruct((2, WIDTH), bf16),...  41 us
    unnamed x1, local copies, waits for them, and re-layouts  1.28 us

profile of v2, /device:TPU:1, one launch (start us, length us, event | category | flops | bytes accessed | tf_op | source)
XLA Modules:
  0.0 43.0 jit_solution(9559083617877228041)
XLA Ops:
  0.7 41.0 %analog_forecast.1 = bf16[2,1024]{1,0:T(2,128)(2,1)} custom-call(bf16[2,1024]{1,0:T(2,128)(2,1)} %queries_hbm.1, bf16[768,1024]{1,0:T(8,128)(2,1)} %keys_hbm.1, bf16[768,1024]{1,0:T(8,128)(2,1)} %futures_hbm.1, s32[1]{0:T(128)S(6)} %copy.7.counts_hbm, s32[4,128]{1,0:T(4,128)} %bitcast.1), custom_call_target="tpu_custom_call" | custom-call | tf_op jit(solution)/shard_map/analog_forecast/pallas_call | solution.py:363
  41.7 1.3 %copy.8 = bf16[2,1024]{1,0:T(2,128)(2,1)} copy(bf16[2,1024]{1,0:T(2,128)(2,1)} %analog_forecast.1) | data formatting | bytes 8192

commit v3 on v2

--- a/solution.py
+++ b/solution.py
@@ -354,6 +354,10 @@
         return carry
 
     lax.fori_loop(0, PLANE, fw_sent, 0)
+
+
+def in_hbm(array):
+    return pltpu.with_memory_space_constraint(array, pltpu.HBM)
 
 
 def body(queries, archive_keys, futures, counts, owners):
@@ -400,10 +404,10 @@
             dma((NZ,)),
         ],
         compiler_params=pltpu.CompilerParams(
-            collective_id=0, has_side_effects=True, vmem_limit_bytes=60 * 2**20
+            collective_id=0, has_side_effects=True, vmem_limit_bytes=40 * 2**20
         ),
         name="analog_forecast",
-    )(queries, archive_keys, futures, counts, owners.reshape(4, 128))
+    )(in_hbm(queries), in_hbm(archive_keys), in_hbm(futures), counts, in_hbm(owners.reshape(4, 128)))
 
 
 def solution(mesh):

time: 43.1 us -> 41.8 us (0.970)
  local copies, waits for them, and re-layouts: 1.28 us -> 0.6 us
  Pallas kernels: 41 us -> 40.4 us
    unnamed x1, local copies, waits for them, and re-layouts: 1.28 us -> 0.6 us
    pallas_call x1, Pallas kernels: 41 us -> 40.4 us  [body(): pl.pallas_call(kernel, out_shape=jax.ShapeDtypeStruct((2, WIDTH), bf16),...]
where the time goes in v3:
time: 41.8 us; the launch traced here: 41.6 us
  Pallas kernels  40.4 us (97%)
  between operations  0.66 us (2%)
  local copies, waits for them, and re-layouts  0.6 us (1%)
    pallas_call x1, Pallas kernels, body(): pl.pallas_call(kernel, out_shape=jax.ShapeDtypeStruct((2, WIDTH), bf16),...  40.4 us

profile of v3, /device:TPU:1, one launch (start us, length us, event | category | flops | bytes accessed | tf_op | source)
XLA Modules:
  0.0 41.6 jit_solution(5695888231725638820)
XLA Ops:
  0.7 40.4 %analog_forecast.1 = bf16[2,1024]{1,0:T(2,128)(2,1)S(1)} custom-call(bf16[2,1024]{1,0:T(2,128)(2,1)} %queries_hbm.1, bf16[768,1024]{1,0:T(8,128)(2,1)} %keys_hbm.1, bf16[768,1024]{1,0:T(8,128)(2,1)} %futures_hbm.1, s32[1]{0:T(128)S(6)} %copy.7.counts_hbm, s32[4,128]{1,0:T(4,128)} %bitcast.1), custom_call_target="tpu_custom_call" | custom-call | tf_op jit(solution)/shard_map/analog_forecast/pallas_call | solution.py:367
  41.0 0.6 %copy.8 = bf16[2,1024]{1,0:T(2,128)(2,1)} copy(bf16[2,1024]{1,0:T(2,128)(2,1)S(1)} %analog_forecast.1) | data formatting | bytes 8192

commit v4 on v3

--- a/solution.py
+++ b/solution.py
@@ -65,6 +65,8 @@
     far_recv,
     near_send,
     near_recv,
+    stat_send,
+    stat_recv,
     zpart_send,
     zpart_recv,
     local_sem,
@@ -78,6 +80,8 @@
     fw_recv,
     ps_send,
     ps_recv,
+    st_send,
+    st_recv,
     zs_send,
     zs_recv,
 ):
@@ -111,8 +115,8 @@
             ]
         )
     ]
-    for load in loads:
-        load.start()
+    loads[0].start()
+    loads[1].start()
 
     barrier = pltpu.get_barrier_semaphore()
     for step in (4, 3, 5, 2, 6, 1, 7):
@@ -123,6 +127,8 @@
     for step in STEPS:
         pl.semaphore_signal(barrier, inc=1, device_id=plane_peer(step)[1], device_id_type=MESH)
     pl.semaphore_signal(barrier, inc=1, device_id=twin, device_id_type=MESH)
+    for load in loads[2:]:
+        load.start()
     loads[0].wait()
     own32[...] = queries[...].astype(jnp.float32)
     loads[1].wait()
@@ -206,7 +212,7 @@
         return remote(block, block, fw_send.at[other], fw_recv.at[other], twin)
 
     fw_copy(plane).start()
-    for step in reversed(STEPS):
+    for step in STEPS:
         other, target = plane_peer(step)
         block = gathered.at[core, other]
         remote(block, block, pg_send.at[0], pg_recv.at[other], target).wait_recv()
@@ -241,12 +247,12 @@
                 (((1,), (1,)), ((), ())),
                 preferred_element_type=jnp.float32,
             )
-            part = jnp.where(column + float(tile * TILE) < limit, part, -1e30)
+            if tile > 0:
+                part = jnp.where(column + float(tile * TILE) < limit, part, -1e30)
             at = half * ARCHIVE + tile * TILE
             scores[:, at : at + TILE] = part
             top = jnp.max(part, axis=1, keepdims=True)
             best = top if best is None else jnp.maximum(best, top)
-    best = best.astype(jnp.bfloat16).astype(jnp.float32)
     total = jnp.zeros((MINE, 1), jnp.float32)
     for tile in range(2 * ARCHIVE // TILE):
         span = slice(tile * TILE, (tile + 1) * TILE)
@@ -254,12 +260,19 @@
         weights[:, span] = weight.astype(jnp.bfloat16)
         total = total + jnp.sum(weight, axis=1, keepdims=True)
 
-    stat_lane = lax.broadcasted_iota(jnp.int32, (1, STATS), 1)
-    high = total.astype(jnp.bfloat16).astype(jnp.float32)
-    stats = jnp.where(stat_lane < 32, best, jnp.where(stat_lane < 64, high, total - high))
-    stats = stats.reshape(2, PLANE, 8, STATS)
-    stats = jnp.stack([stats[0], stats[1]], axis=1).reshape(MINE, STATS)
-    far_send[:, :, HALF:] = stats.astype(jnp.bfloat16).reshape(PLANE, ROWS, STATS)
+    stat_lane = lax.broadcasted_iota(jnp.int32, (MINE, STATS), 1)
+    stat_row = lax.broadcasted_iota(jnp.int32, (MINE, STATS), 0)
+    stat_here = stat_lane == (stat_row // GROUP) * 8 + stat_row % 8
+    for k, value in enumerate((best, total)):
+        value = jnp.where(stat_here, value, 0.0).reshape(2, PLANE, 8, STATS)
+        stat_send[:, k : k + 1, :] = jnp.sum(value[0] + value[1], axis=1, keepdims=True)
+    st_sends = []
+    for k, step in enumerate(STEPS):
+        other, target = plane_peer(step)
+        copy = remote(stat_send.at[other], stat_recv.at[plane], st_send.at[k], st_recv.at[plane], target)
+        copy.start()
+        st_sends.append(copy)
+    stat_recv[plane] = stat_send[plane]
 
     ps_sends = []
     for group, (send, recv) in enumerate(((far_send, far_recv), (near_send, near_recv))):
@@ -276,7 +289,7 @@
                 sums = term if sums is None else sums + term
             halves.append(sums.reshape(PLANE, 8, HALF))
         sums = jnp.stack(halves, axis=1).reshape(MINE, HALF)
-        send[:, :, :HALF] = sums.astype(jnp.bfloat16).reshape(PLANE, ROWS, HALF)
+        send[...] = sums.astype(jnp.bfloat16).reshape(PLANE, ROWS, HALF)
         for k, step in enumerate(STEPS):
             other, target = plane_peer(step)
             copy = remote(send.at[other], recv.at[plane], ps_send.at[group, k], ps_recv.at[group, plane], target)
@@ -284,26 +297,36 @@
             ps_sends.append(copy)
         recv[plane] = send[plane]
 
+    for step in STEPS:
+        other, target = plane_peer(step)
+        remote(stat_send.at[other], stat_recv.at[other], st_send.at[0], st_recv.at[other], target).wait_recv()
+    at_row = lax.broadcasted_iota(jnp.int32, (ROWS, STATS), 0) == lax.broadcasted_iota(jnp.int32, (ROWS, STATS), 1)
+
+    def upright(value):
+        return jnp.sum(jnp.where(at_row, value, 0.0), axis=1, keepdims=True)
+
+    maxima = [stat_recv[k, 0:1, :] for k in range(PLANE)]
+    best = maxima[0]
+    for k in range(1, PLANE):
+        best = jnp.maximum(best, maxima[k])
+    scales = [jnp.exp2((m - best) * exponent_factor) for m in maxima]
+    total = jnp.zeros((1, STATS), jnp.float32)
+    for k in range(PLANE):
+        total = total + stat_recv[k, 1:2, :] * scales[k]
+    scales = [upright(scale) for scale in scales]
+    passed_lane = lax.broadcasted_iota(jnp.int32, (1, STATS), 1)
+    passed = jnp.where(passed_lane < 64, upright(best), upright(total))
+
     zs_sends = []
     for group, (send, recv) in enumerate(((far_send, far_recv), (near_send, near_recv))):
         for step in STEPS:
             other, target = plane_peer(step)
             remote(send.at[other], recv.at[other], ps_send.at[group, 0], ps_recv.at[group, other], target).wait_recv()
-        if group == 0:
-            stats = [recv[k, :, HALF:].astype(jnp.float32) for k in range(PLANE)]
-            best = stats[0][:, 0:1]
-            for k in range(1, PLANE):
-                best = jnp.maximum(best, stats[k][:, 0:1])
-            scales = [jnp.exp2((s[:, 0:1] - best) * exponent_factor) for s in stats]
-            total = jnp.zeros((ROWS, 1), jnp.float32)
-            for k in range(PLANE):
-                total = total + (stats[k][:, 32:33] + stats[k][:, 64:65]) * scales[k]
-            passed = jnp.where(stat_lane < 64, best, total)
         sums = jnp.zeros((ROWS, HALF), jnp.float32)
         for k in range(PLANE):
             scale = scales[k][group * 8 : group * 8 + 8]
             scale = jnp.concatenate([scale, scale], axis=0)
-            sums = sums + recv[k, :, :HALF].astype(jnp.float32) * scale
+            sums = sums + recv[k].astype(jnp.float32) * scale
         for index, offset in enumerate(OFFSETS[1 - group]):
             slot = group * 4 + index
             zpart_send[slot, :, :HALF] = sums[2 * index : 2 * index + 2, :]
@@ -342,7 +365,7 @@
     norm_factor = lax.rsqrt(jnp.mean(analog * analog, axis=1, keepdims=True) + 1e-06)
     out[...] = (analog * norm_factor).astype(jnp.bfloat16)
 
-    for copy in zg_sends + pg_sends + ps_sends + zs_sends:
+    for copy in zg_sends + pg_sends + st_sends + ps_sends + zs_sends:
         copy.wait_send()
 
     @pl.when(core == 1)
@@ -383,10 +406,12 @@
             pltpu.VMEM((2, MINE, MINE), bf16),
             pltpu.VMEM((MINE, 2 * ARCHIVE), f32),
             pltpu.VMEM((MINE, 2 * ARCHIVE), bf16),
-            pltpu.VMEM((PLANE, ROWS, HALF + STATS), bf16),
-            pltpu.VMEM((PLANE, ROWS, HALF + STATS), bf16),
             pltpu.VMEM((PLANE, ROWS, HALF), bf16),
             pltpu.VMEM((PLANE, ROWS, HALF), bf16),
+            pltpu.VMEM((PLANE, ROWS, HALF), bf16),
+            pltpu.VMEM((PLANE, ROWS, HALF), bf16),
+            pltpu.VMEM((PLANE, 2, STATS), f32),
+            pltpu.VMEM((PLANE, 2, STATS), f32),
             pltpu.VMEM((NZ, 2, WIDTH + STATS), f32),
             pltpu.VMEM((NZ, 2, WIDTH + STATS), f32),
             dma((5,)),
@@ -400,6 +425,8 @@
             dma((PLANE,)),
             dma((2, PLANE)),
             dma((2, PLANE)),
+            dma((PLANE,)),
+            dma((PLANE,)),
             dma((NZ,)),
             dma((NZ,)),
         ],

time: 41.8 us -> 41.4 us (level)
  no operation moved by 1% of the time
where the time goes in v4:
time: 41.4 us; the launch traced here: 41.3 us
  Pallas kernels  40 us (97%)
  between operations  0.66 us (2%)
  local copies, waits for them, and re-layouts  0.6 us (1%)
    pallas_call x1, Pallas kernels, body(): pl.pallas_call(kernel, out_shape=jax.ShapeDtypeStruct((2, WIDTH), bf16),...  40 us

profile of v4, /device:TPU:1, one launch (start us, length us, event | category | flops | bytes accessed | tf_op | source)
XLA Modules:
  0.0 41.3 jit_solution(13773905281827338549)
XLA Ops:
  0.7 40.0 %analog_forecast.1 = bf16[2,1024]{1,0:T(2,128)(2,1)S(1)} custom-call(bf16[2,1024]{1,0:T(2,128)(2,1)} %queries_hbm.1, bf16[768,1024]{1,0:T(8,128)(2,1)} %keys_hbm.1, bf16[768,1024]{1,0:T(8,128)(2,1)} %futures_hbm.1, s32[1]{0:T(128)S(6)} %copy.7.counts_hbm, s32[4,128]{1,0:T(4,128)} %bitcast.1), custom_call_target="tpu_custom_call" | custom-call | tf_op jit(solution)/shard_map/analog_forecast/pallas_call | solution.py:390
  40.7 0.6 %copy.8 = bf16[2,1024]{1,0:T(2,128)(2,1)} copy(bf16[2,1024]{1,0:T(2,128)(2,1)S(1)} %analog_forecast.1) | data formatting | bytes 8192

commit v5 on v4

--- a/solution.py
+++ b/solution.py
@@ -61,10 +61,10 @@
     onehot,
     scores,
     weights,
-    far_send,
-    far_recv,
-    near_send,
-    near_recv,
+    low_send,
+    low_recv,
+    high_send,
+    high_recv,
     stat_send,
     stat_recv,
     zpart_send,
@@ -168,7 +168,7 @@
     lane = lax.broadcasted_iota(jnp.int32, (32, 128), 1)
     row = lax.broadcasted_iota(jnp.int32, (32, 128), 0)
     for group in range(2):
-        wanted = natural_row(0, row // 8, (z + pick((row // 2) % 4, OFFSETS[1 - group])) % NZ, core, row % 2)
+        wanted = natural_row(0, row // 8, group * 4 + (row // 2) % 4, core, row % 2)
         for block in range(NX):
             picked = jnp.where(lane == wanted, owners[block : block + 1, :].astype(jnp.float32), 0.0)
             owner = jnp.sum(picked, axis=1, keepdims=True)
@@ -275,7 +275,7 @@
     stat_recv[plane] = stat_send[plane]
 
     ps_sends = []
-    for group, (send, recv) in enumerate(((far_send, far_recv), (near_send, near_recv))):
+    for group, (send, recv) in enumerate(((low_send, low_recv), (high_send, high_recv))):
         halves = []
         for half in range(2):
             span = slice(half * HALF, (half + 1) * HALF)
@@ -317,8 +317,17 @@
     passed_lane = lax.broadcasted_iota(jnp.int32, (1, STATS), 1)
     passed = jnp.where(passed_lane < 64, upright(best), upright(total))
 
-    zs_sends = []
-    for group, (send, recv) in enumerate(((far_send, far_recv), (near_send, near_recv))):
+    def zs_copy(group, step):
+        other = group * 4 + (z + step) % 4
+        return remote(
+            zpart_send.at[other],
+            zpart_recv.at[z],
+            zs_send.at[other],
+            zs_recv.at[z],
+            device(x, y, other, core),
+        )
+
+    for group, (send, recv) in enumerate(((low_send, low_recv), (high_send, high_recv))):
         for step in STEPS:
             other, target = plane_peer(step)
             remote(send.at[other], recv.at[other], ps_send.at[group, 0], ps_recv.at[group, other], target).wait_recv()
@@ -327,25 +336,21 @@
             scale = scales[k][group * 8 : group * 8 + 8]
             scale = jnp.concatenate([scale, scale], axis=0)
             sums = sums + recv[k].astype(jnp.float32) * scale
-        for index, offset in enumerate(OFFSETS[1 - group]):
+        for index in range(4):
             slot = group * 4 + index
             zpart_send[slot, :, :HALF] = sums[2 * index : 2 * index + 2, :]
             zpart_send[slot, :, HALF:WIDTH] = sums[8 + 2 * index : 8 + 2 * index + 2, :]
             zpart_send[slot, :, WIDTH:] = passed[group * 8 + 2 * index : group * 8 + 2 * index + 2, :]
-        for index, offset in enumerate(OFFSETS[1 - group]):
-            slot = group * 4 + index
-            if offset == 0:
-                zpart_recv[z] = zpart_send[slot]
-            else:
-                copy = remote(
-                    zpart_send.at[slot],
-                    zpart_recv.at[z],
-                    zs_send.at[offset],
-                    zs_recv.at[z],
-                    device(x, y, (z + offset) % NZ, core),
-                )
-                copy.start()
-                zs_sends.append(copy)
+        for step in range(3, 0, -1):
+            zs_copy(group, step).start()
+
+        @pl.when(z // 4 == group)
+        def _():
+            zpart_recv[z] = zpart_send[z]
+
+        @pl.when(z // 4 != group)
+        def _():
+            zs_copy(group, 0).start()
 
     for step in range(1, NZ):
         other = (z + step) % NZ
@@ -365,8 +370,15 @@
     norm_factor = lax.rsqrt(jnp.mean(analog * analog, axis=1, keepdims=True) + 1e-06)
     out[...] = (analog * norm_factor).astype(jnp.bfloat16)
 
-    for copy in zg_sends + pg_sends + st_sends + ps_sends + zs_sends:
+    for copy in zg_sends + pg_sends + st_sends + ps_sends:
         copy.wait_send()
+    for group in range(2):
+        for step in range(1, 4):
+            zs_copy(group, step).wait_send()
+
+        @pl.when(z // 4 != group)
+        def _():
+            zs_copy(group, 0).wait_send()
 
     @pl.when(core == 1)
     def _():

time: 41.4 us -> 40.4 us (0.976)
  Pallas kernels: 40 us -> 39 us
    pallas_call x1, Pallas kernels: 40 us -> 39 us  [body(): pl.pallas_call(kernel, out_shape=jax.ShapeDtypeStruct((2, WIDTH), bf16),...]
where the time goes in v5:
time: 40.4 us; the launch traced here: 40.3 us
  Pallas kernels  39 us (97%)
  between operations  0.66 us (2%)
  local copies, waits for them, and re-layouts  0.6 us (1%)
    pallas_call x1, Pallas kernels, body(): pl.pallas_call(kernel, out_shape=jax.ShapeDtypeStruct((2, WIDTH), bf16),...  39 us

profile of v5, /device:TPU:1, one launch (start us, length us, event | category | flops | bytes accessed | tf_op | source)
XLA Modules:
  0.0 40.3 jit_solution(4994540767679531320)
XLA Ops:
  0.7 39.0 %analog_forecast.1 = bf16[2,1024]{1,0:T(2,128)(2,1)S(1)} custom-call(bf16[2,1024]{1,0:T(2,128)(2,1)} %queries_hbm.1, bf16[768,1024]{1,0:T(8,128)(2,1)} %keys_hbm.1, bf16[768,1024]{1,0:T(8,128)(2,1)} %futures_hbm.1, s32[1]{0:T(128)S(6)} %copy.7.counts_hbm, s32[4,128]{1,0:T(4,128)} %bitcast.1), custom_call_target="tpu_custom_call" | custom-call | tf_op jit(solution)/shard_map/analog_forecast/pallas_call | solution.py:402
  39.7 0.6 %copy.8 = bf16[2,1024]{1,0:T(2,128)(2,1)} copy(bf16[2,1024]{1,0:T(2,128)(2,1)S(1)} %analog_forecast.1) | data formatting | bytes 8192

commit v6 on v5

--- a/solution.py
+++ b/solution.py
@@ -56,6 +56,7 @@
     gather32,
     gathered,
     keys,
+    upright_keys,
     futures,
     limits,
     onehot,
@@ -185,6 +186,14 @@
                     owner == held.astype(jnp.float32), 1.0, 0.0
                 ).astype(jnp.bfloat16)
 
+    def turn_keys(side):
+        for tile in range(ARCHIVE // TILE):
+            at = side * ARCHIVE + tile * TILE
+            upright_keys[:, at : at + TILE] = keys[side, tile * TILE : (tile + 1) * TILE, :].T
+
+    loads[3].wait()
+    turn_keys(0)
+
     def zg_wait(slot):
         remote(own32, zgather.at[slot], zg_send.at[0], zg_recv.at[slot], twin).wait_recv()
 
@@ -212,6 +221,10 @@
         return remote(block, block, fw_send.at[other], fw_recv.at[other], twin)
 
     fw_copy(plane).start()
+    loads[4].wait()
+    for copy in to_twin:
+        copy.wait()
+    turn_keys(1)
     for step in STEPS:
         other, target = plane_peer(step)
         block = gathered.at[core, other]
@@ -221,10 +234,6 @@
     every = gathered[core].reshape(MINE, WIDTH)
     mine = jnp.dot(onehot[core], every, preferred_element_type=jnp.float32)
 
-    for load in loads[3:]:
-        load.wait()
-    for copy in to_twin:
-        copy.wait()
 
     def fw_wait(other, carry):
         block = gathered.at[1 - core, other]
@@ -237,52 +246,59 @@
     mine = (mine + jnp.dot(onehot[1 - core], every, preferred_element_type=jnp.float32)).astype(jnp.bfloat16)
 
     column = lax.broadcasted_iota(jnp.int32, (1, TILE), 1).astype(jnp.float32)
-    best = None
-    for half in range(2):
-        limit = limits[half, 0:1, 0:1]
-        for tile in range(ARCHIVE // TILE):
-            part = lax.dot_general(
-                mine,
-                keys[half, tile * TILE : (tile + 1) * TILE, :],
-                (((1,), (1,)), ((), ())),
-                preferred_element_type=jnp.float32,
+    def score(group):
+        for side in range(2):
+            limit = limits[side, 0:1, 0:1]
+            for tile in range(ARCHIVE // TILE):
+                at = side * ARCHIVE + tile * TILE
+                part = jnp.dot(
+                    mine[group * GROUP : (group + 1) * GROUP],
+                    upright_keys[:, at : at + TILE],
+                    preferred_element_type=jnp.float32,
+                )
+                if tile > 0:
+                    part = jnp.where(column + float(tile * TILE) < limit, part, -1e30)
+                scores[group, :, at : at + TILE] = part
+
+    def softmax(group):
+        best = None
+        for tile in range(2 * ARCHIVE // TILE):
+            top = jnp.max(scores[group, :, tile * TILE : (tile + 1) * TILE], axis=1, keepdims=True)
+            best = top if best is None else jnp.maximum(best, top)
+        total = jnp.zeros((GROUP, 1), jnp.float32)
+        for tile in range(2 * ARCHIVE // TILE):
+            span = slice(tile * TILE, (tile + 1) * TILE)
+            weight = jnp.exp2((scores[group, :, span] - best) * exponent_factor)
+            weights[group, :, span] = weight.astype(jnp.bfloat16)
+            total = total + jnp.sum(weight, axis=1, keepdims=True)
+        return best, total
+
+    here = lax.broadcasted_iota(jnp.int32, (GROUP, STATS), 0) % 8 == lax.broadcasted_iota(jnp.int32, (GROUP, STATS), 1)
+    ps_sends, st_sends = [], []
+    for group, (send, recv) in enumerate(((low_send, low_recv), (high_send, high_recv))):
+        score(group)
+        for k, value in enumerate(softmax(group)):
+            value = jnp.where(here, value, 0.0).reshape(PLANE, 8, STATS)
+            stat_send[group, :, k : k + 1, :] = jnp.sum(value, axis=1, keepdims=True)
+        for k, step in enumerate(STEPS):
+            other, target = plane_peer(step)
+            copy = remote(
+                stat_send.at[group, other],
+                stat_recv.at[group, plane],
+                st_send.at[group, k],
+                st_recv.at[group, plane],
+                target,
             )
-            if tile > 0:
-                part = jnp.where(column + float(tile * TILE) < limit, part, -1e30)
-            at = half * ARCHIVE + tile * TILE
-            scores[:, at : at + TILE] = part
-            top = jnp.max(part, axis=1, keepdims=True)
-            best = top if best is None else jnp.maximum(best, top)
-    total = jnp.zeros((MINE, 1), jnp.float32)
-    for tile in range(2 * ARCHIVE // TILE):
-        span = slice(tile * TILE, (tile + 1) * TILE)
-        weight = jnp.exp2((scores[:, span] - best) * exponent_factor)
-        weights[:, span] = weight.astype(jnp.bfloat16)
-        total = total + jnp.sum(weight, axis=1, keepdims=True)
-
-    stat_lane = lax.broadcasted_iota(jnp.int32, (MINE, STATS), 1)
-    stat_row = lax.broadcasted_iota(jnp.int32, (MINE, STATS), 0)
-    stat_here = stat_lane == (stat_row // GROUP) * 8 + stat_row % 8
-    for k, value in enumerate((best, total)):
-        value = jnp.where(stat_here, value, 0.0).reshape(2, PLANE, 8, STATS)
-        stat_send[:, k : k + 1, :] = jnp.sum(value[0] + value[1], axis=1, keepdims=True)
-    st_sends = []
-    for k, step in enumerate(STEPS):
-        other, target = plane_peer(step)
-        copy = remote(stat_send.at[other], stat_recv.at[plane], st_send.at[k], st_recv.at[plane], target)
-        copy.start()
-        st_sends.append(copy)
-    stat_recv[plane] = stat_send[plane]
-
-    ps_sends = []
-    for group, (send, recv) in enumerate(((low_send, low_recv), (high_send, high_recv))):
+            copy.start()
+            st_sends.append(copy)
+        stat_recv[group, plane] = stat_send[group, plane]
         halves = []
         for half in range(2):
             span = slice(half * HALF, (half + 1) * HALF)
             sums = None
             for side in range(2):
                 term = jnp.dot(
-                    weights[group * GROUP : (group + 1) * GROUP, side * ARCHIVE : (side + 1) * ARCHIVE],
+                    weights[group, :, side * ARCHIVE : (side + 1) * ARCHIVE],
                     futures[side, :, span],
                     preferred_element_type=jnp.float32,
                 )
@@ -297,26 +313,25 @@
             ps_sends.append(copy)
         recv[plane] = send[plane]
 
-    for step in STEPS:
-        other, target = plane_peer(step)
-        remote(stat_send.at[other], stat_recv.at[other], st_send.at[0], st_recv.at[other], target).wait_recv()
-    at_row = lax.broadcasted_iota(jnp.int32, (ROWS, STATS), 0) == lax.broadcasted_iota(jnp.int32, (ROWS, STATS), 1)
+    for copy in zg_sends + pg_sends:
+        copy.wait_send()
+
+    @pl.when(core == 1)
+    def _():
+        to_core0.wait_send()
+
+    def fw_sent(other, carry):
+        fw_copy(other).wait_send()
+        return carry
+
+    lax.fori_loop(0, PLANE, fw_sent, 0)
+
+    at_row = lax.broadcasted_iota(jnp.int32, (8, STATS), 0) == lax.broadcasted_iota(jnp.int32, (8, STATS), 1)
 
     def upright(value):
         return jnp.sum(jnp.where(at_row, value, 0.0), axis=1, keepdims=True)
 
-    maxima = [stat_recv[k, 0:1, :] for k in range(PLANE)]
-    best = maxima[0]
-    for k in range(1, PLANE):
-        best = jnp.maximum(best, maxima[k])
-    scales = [jnp.exp2((m - best) * exponent_factor) for m in maxima]
-    total = jnp.zeros((1, STATS), jnp.float32)
-    for k in range(PLANE):
-        total = total + stat_recv[k, 1:2, :] * scales[k]
-    scales = [upright(scale) for scale in scales]
     passed_lane = lax.broadcasted_iota(jnp.int32, (1, STATS), 1)
-    passed = jnp.where(passed_lane < 64, upright(best), upright(total))
-
     def zs_copy(group, step):
         other = group * 4 + (z + step) % 4
         return remote(
@@ -330,17 +345,35 @@
     for group, (send, recv) in enumerate(((low_send, low_recv), (high_send, high_recv))):
         for step in STEPS:
             other, target = plane_peer(step)
+            remote(
+                stat_send.at[group, other],
+                stat_recv.at[group, other],
+                st_send.at[group, 0],
+                st_recv.at[group, other],
+                target,
+            ).wait_recv()
+        maxima = [stat_recv[group, k, 0:1, :] for k in range(PLANE)]
+        best = maxima[0]
+        for k in range(1, PLANE):
+            best = jnp.maximum(best, maxima[k])
+        scales = [jnp.exp2((m - best) * exponent_factor) for m in maxima]
+        total = jnp.zeros((1, STATS), jnp.float32)
+        for k in range(PLANE):
+            total = total + stat_recv[group, k, 1:2, :] * scales[k]
+        scales = [upright(scale) for scale in scales]
+        passed = jnp.where(passed_lane < 64, upright(best), upright(total))
+        for step in STEPS:
+            other, target = plane_peer(step)
             remote(send.at[other], recv.at[other], ps_send.at[group, 0], ps_recv.at[group, other], target).wait_recv()
         sums = jnp.zeros((ROWS, HALF), jnp.float32)
         for k in range(PLANE):
-            scale = scales[k][group * 8 : group * 8 + 8]
-            scale = jnp.concatenate([scale, scale], axis=0)
+            scale = jnp.concatenate([scales[k], scales[k]], axis=0)
             sums = sums + recv[k].astype(jnp.float32) * scale
         for index in range(4):
             slot = group * 4 + index
             zpart_send[slot, :, :HALF] = sums[2 * index : 2 * index + 2, :]
             zpart_send[slot, :, HALF:WIDTH] = sums[8 + 2 * index : 8 + 2 * index + 2, :]
-            zpart_send[slot, :, WIDTH:] = passed[group * 8 + 2 * index : group * 8 + 2 * index + 2, :]
+            zpart_send[slot, :, WIDTH:] = passed[2 * index : 2 * index + 2, :]
         for step in range(3, 0, -1):
             zs_copy(group, step).start()
 
@@ -351,6 +384,9 @@
         @pl.when(z // 4 != group)
         def _():
             zs_copy(group, 0).start()
+
+    for copy in st_sends + ps_sends:
+        copy.wait_send()
 
     for step in range(1, NZ):
         other = (z + step) % NZ
@@ -370,8 +406,6 @@
     norm_factor = lax.rsqrt(jnp.mean(analog * analog, axis=1, keepdims=True) + 1e-06)
     out[...] = (analog * norm_factor).astype(jnp.bfloat16)
 
-    for copy in zg_sends + pg_sends + st_sends + ps_sends:
-        copy.wait_send()
     for group in range(2):
         for step in range(1, 4):
             zs_copy(group, step).wait_send()
@@ -379,16 +413,6 @@
         @pl.when(z // 4 != group)
         def _():
             zs_copy(group, 0).wait_send()
-
-    @pl.when(core == 1)
-    def _():
-        to_core0.wait_send()
-
-    def fw_sent(other, carry):
-        fw_copy(other).wait_send()
-        return carry
-
-    lax.fori_loop(0, PLANE, fw_sent, 0)
 
 
 def in_hbm(array):
@@ -413,17 +437,18 @@
             pltpu.VMEM((ROWS, WIDTH), f32),
             pltpu.VMEM((2, PLANE, ROWS, WIDTH), bf16),
             pltpu.VMEM((2, ARCHIVE, WIDTH), bf16),
+            pltpu.VMEM((WIDTH, 2 * ARCHIVE), bf16),
             pltpu.VMEM((2, ARCHIVE, WIDTH), bf16),
             pltpu.VMEM((2, 8, 128), f32),
             pltpu.VMEM((2, MINE, MINE), bf16),
-            pltpu.VMEM((MINE, 2 * ARCHIVE), f32),
-            pltpu.VMEM((MINE, 2 * ARCHIVE), bf16),
+            pltpu.VMEM((2, GROUP, 2 * ARCHIVE), f32),
+            pltpu.VMEM((2, GROUP, 2 * ARCHIVE), bf16),
             pltpu.VMEM((PLANE, ROWS, HALF), bf16),
             pltpu.VMEM((PLANE, ROWS, HALF), bf16),
             pltpu.VMEM((PLANE, ROWS, HALF), bf16),
             pltpu.VMEM((PLANE, ROWS, HALF), bf16),
-            pltpu.VMEM((PLANE, 2, STATS), f32),
-            pltpu.VMEM((PLANE, 2, STATS), f32),
+            pltpu.VMEM((2, PLANE, 2, STATS), f32),
+            pltpu.VMEM((2, PLANE, 2, STATS), f32),
             pltpu.VMEM((NZ, 2, WIDTH + STATS), f32),
             pltpu.VMEM((NZ, 2, WIDTH + STATS), f32),
             dma((5,)),
@@ -437,8 +462,8 @@
             dma((PLANE,)),
             dma((2, PLANE)),
             dma((2, PLANE)),
-            dma((PLANE,)),
-            dma((PLANE,)),
+            dma((2, PLANE)),
+            dma((2, PLANE)),
             dma((NZ,)),
             dma((NZ,)),
         ],

time: 40.4 us -> 40.2 us (level)
  no operation moved by 1% of the time
where the time goes in v6:
time: 40.2 us; the launch traced here: 40.1 us
  Pallas kernels  38.8 us (97%)
  between operations  0.66 us (2%)
  local copies, waits for them, and re-layouts  0.6 us (1%)
    pallas_call x1, Pallas kernels, body(): pl.pallas_call(kernel, out_shape=jax.ShapeDtypeStruct((2, WIDTH), bf16),...  38.8 us

profile of v6, /device:TPU:1, one launch (start us, length us, event | category | flops | bytes accessed | tf_op | source)
XLA Modules:
  0.0 40.1 jit_solution(7888385687518727306)
XLA Ops:
  0.7 38.8 %analog_forecast.1 = bf16[2,1024]{1,0:T(2,128)(2,1)S(1)} custom-call(bf16[2,1024]{1,0:T(2,128)(2,1)} %queries_hbm.1, bf16[768,1024]{1,0:T(8,128)(2,1)} %keys_hbm.1, bf16[768,1024]{1,0:T(8,128)(2,1)} %futures_hbm.1, s32[1]{0:T(128)S(6)} %copy.7.counts_hbm, s32[4,128]{1,0:T(4,128)} %bitcast.1), custom_call_target="tpu_custom_call" | custom-call | tf_op jit(solution)/shard_map/analog_forecast/pallas_call | solution.py:426
  39.5 0.6 %copy.8 = bf16[2,1024]{1,0:T(2,128)(2,1)} copy(bf16[2,1024]{1,0:T(2,128)(2,1)S(1)} %analog_forecast.1) | data formatting | bytes 8192

commit v7 on v6

--- a/solution.py
+++ b/solution.py
@@ -18,8 +18,7 @@
 ARCHIVE = 768
 TILE = 256
 
-NEAR, FAR = (0, 1, 7, 6), (4, 3, 5, 2)
-OFFSETS = NEAR, FAR
+OFFSETS = (0, 1, 2, 3), (4, 5, 6, 7)
 
 STEPS = sorted(
     [(a, b) for a in range(NX) for b in range(NY) if a or b],
@@ -139,7 +138,7 @@
     zg_sends = []
     for step in (4, 3, 5, 2, 6, 1, 7):
         offset = (NZ - step) % NZ
-        side = 0 if offset in NEAR else 1
+        side = 0 if offset in OFFSETS[0] else 1
         slot = OFFSETS[side].index(offset) * 2 + core
         copy = remote(
             own32, zgather.at[slot], zg_send.at[step], zg_recv.at[slot], device(x, y, (z + step) % NZ, side)

time: 40.2 us -> 39.6 us (0.985)
  Pallas kernels: 38.8 us -> 38.2 us
    pallas_call x1, Pallas kernels: 38.8 us -> 38.2 us  [body(): pl.pallas_call(kernel, out_shape=jax.ShapeDtypeStruct((2, WIDTH), bf16),...]
where the time goes in v7:
time: 39.6 us; the launch traced here: 39.5 us
  Pallas kernels  38.2 us (96%)
  between operations  0.66 us (2%)
  local copies, waits for them, and re-layouts  0.6 us (2%)
    pallas_call x1, Pallas kernels, body(): pl.pallas_call(kernel, out_shape=jax.ShapeDtypeStruct((2, WIDTH), bf16),...  38.2 us

profile of v7, /device:TPU:1, one launch (start us, length us, event | category | flops | bytes accessed | tf_op | source)
XLA Modules:
  0.0 39.5 jit_solution(18425366903122002992)
XLA Ops:
  0.7 38.2 %analog_forecast.1 = bf16[2,1024]{1,0:T(2,128)(2,1)S(1)} custom-call(bf16[2,1024]{1,0:T(2,128)(2,1)} %queries_hbm.1, bf16[768,1024]{1,0:T(8,128)(2,1)} %keys_hbm.1, bf16[768,1024]{1,0:T(8,128)(2,1)} %futures_hbm.1, s32[1]{0:T(128)S(6)} %copy.7.counts_hbm, s32[4,128]{1,0:T(4,128)} %bitcast.1), custom_call_target="tpu_custom_call" | custom-call | tf_op jit(solution)/shard_map/analog_forecast/pallas_call | solution.py:425
  38.9 0.6 %copy.8 = bf16[2,1024]{1,0:T(2,128)(2,1)} copy(bf16[2,1024]{1,0:T(2,128)(2,1)S(1)} %analog_forecast.1) | data formatting | bytes 8192

commit v8 on v7

--- a/solution.py
+++ b/solution.py
@@ -359,15 +359,17 @@
         total = jnp.zeros((1, STATS), jnp.float32)
         for k in range(PLANE):
             total = total + stat_recv[group, k, 1:2, :] * scales[k]
-        scales = [upright(scale) for scale in scales]
         passed = jnp.where(passed_lane < 64, upright(best), upright(total))
-        for step in STEPS:
+        def column(other):
+            scale = upright(jnp.exp2((stat_recv[group, other, 0:1, :] - best) * exponent_factor))
+            return jnp.concatenate([scale, scale], axis=0)
+
+        columns = [column(plane_peer(step)[0]) for step in STEPS]
+        sums = recv[plane].astype(jnp.float32) * column(plane)
+        for step, scale in zip(STEPS, columns):
             other, target = plane_peer(step)
             remote(send.at[other], recv.at[other], ps_send.at[group, 0], ps_recv.at[group, other], target).wait_recv()
-        sums = jnp.zeros((ROWS, HALF), jnp.float32)
-        for k in range(PLANE):
-            scale = jnp.concatenate([scales[k], scales[k]], axis=0)
-            sums = sums + recv[k].astype(jnp.float32) * scale
+            sums = sums + recv[other].astype(jnp.float32) * scale
         for index in range(4):
             slot = group * 4 + index
             zpart_send[slot, :, :HALF] = sums[2 * index : 2 * index + 2, :]

time: 39.6 us -> 40.6 us (1.025)
  Pallas kernels: 38.2 us -> 39.2 us
    pallas_call x1, Pallas kernels: 38.2 us -> 39.2 us  [body(): pl.pallas_call(kernel, out_shape=jax.ShapeDtypeStruct((2, WIDTH), bf16),...]
where the time goes in v8:
time: 40.6 us; the launch traced here: 40.5 us
  Pallas kernels  39.2 us (97%)
  between operations  0.66 us (2%)
  local copies, waits for them, and re-layouts  0.6 us (1%)
    pallas_call x1, Pallas kernels, body(): pl.pallas_call(kernel, out_shape=jax.ShapeDtypeStruct((2, WIDTH), bf16),...  39.2 us

profile of v8, /device:TPU:1, one launch (start us, length us, event | category | flops | bytes accessed | tf_op | source)
XLA Modules:
  0.0 40.5 jit_solution(4222593417401074800)
XLA Ops:
  0.7 39.2 %analog_forecast.1 = bf16[2,1024]{1,0:T(2,128)(2,1)S(1)} custom-call(bf16[2,1024]{1,0:T(2,128)(2,1)} %queries_hbm.1, bf16[768,1024]{1,0:T(8,128)(2,1)} %keys_hbm.1, bf16[768,1024]{1,0:T(8,128)(2,1)} %futures_hbm.1, s32[1]{0:T(128)S(6)} %copy.7.counts_hbm, s32[4,128]{1,0:T(4,128)} %bitcast.1), custom_call_target="tpu_custom_call" | custom-call | tf_op jit(solution)/shard_map/analog_forecast/pallas_call | solution.py:427
  39.9 0.6 %copy.8 = bf16[2,1024]{1,0:T(2,128)(2,1)} copy(bf16[2,1024]{1,0:T(2,128)(2,1)S(1)} %analog_forecast.1) | data formatting | bytes 8192

commit v9 on v7

--- a/solution.py
+++ b/solution.py
@@ -373,16 +373,16 @@
             zpart_send[slot, :, :HALF] = sums[2 * index : 2 * index + 2, :]
             zpart_send[slot, :, HALF:WIDTH] = sums[8 + 2 * index : 8 + 2 * index + 2, :]
             zpart_send[slot, :, WIDTH:] = passed[2 * index : 2 * index + 2, :]
+        @pl.when(z // 4 != group)
+        def _():
+            zs_copy(group, 0).start()
+
         for step in range(3, 0, -1):
             zs_copy(group, step).start()
 
         @pl.when(z // 4 == group)
         def _():
             zpart_recv[z] = zpart_send[z]
-
-        @pl.when(z // 4 != group)
-        def _():
-            zs_copy(group, 0).start()
 
     for copy in st_sends + ps_sends:
         copy.wait_send()

time: 39.6 us -> 39.6 us (level)
  no operation moved by 1% of the time
where the time goes in v9:
time: 39.6 us; the launch traced here: 39.5 us
  Pallas kernels  38.2 us (96%)
  between operations  0.66 us (2%)
  local copies, waits for them, and re-layouts  0.6 us (2%)
    pallas_call x1, Pallas kernels, body(): pl.pallas_call(kernel, out_shape=jax.ShapeDtypeStruct((2, WIDTH), bf16),...  38.2 us

profile of v9, /device:TPU:1, one launch (start us, length us, event | category | flops | bytes accessed | tf_op | source)
XLA Modules:
  0.0 39.5 jit_solution(17231749616957556474)
XLA Ops:
  0.7 38.2 %analog_forecast.1 = bf16[2,1024]{1,0:T(2,128)(2,1)S(1)} custom-call(bf16[2,1024]{1,0:T(2,128)(2,1)} %queries_hbm.1, bf16[768,1024]{1,0:T(8,128)(2,1)} %keys_hbm.1, bf16[768,1024]{1,0:T(8,128)(2,1)} %futures_hbm.1, s32[1]{0:T(128)S(6)} %copy.7.counts_hbm, s32[4,128]{1,0:T(4,128)} %bitcast.1), custom_call_target="tpu_custom_call" | custom-call | tf_op jit(solution)/shard_map/analog_forecast/pallas_call | solution.py:425
  38.9 0.6 %copy.8 = bf16[2,1024]{1,0:T(2,128)(2,1)} copy(bf16[2,1024]{1,0:T(2,128)(2,1)S(1)} %analog_forecast.1) | data formatting | bytes 8192
